TPU v7x, 32 devices: a whole 2x2x4 slice. The times are simulated.
32 devices in a mesh: lat: 4 (over y, x), lon: 8 (over z, core).
Axes of the slice: x: 2, y: 2, z: 4, core: 2. Of those that a mesh axis runs over, the one named last changes fastest.
Arguments:
- background: bfloat16 [64, 256, 512], P('lat', 'lon'), may hold values from -6 to 6
- observations: bfloat16 [32768, 256], P(('lat', 'lon')), may hold values from -6 to 6
- destination: int32 [32768, 1], P(('lat', 'lon')), may hold values from 0 to 31; in each aligned block of 1024 rows (0 to 1023, 1024 to 2047, ...) at most 64 rows name the same one
- footprint: int32 [32768, 4], P(('lat', 'lon')), may hold values from 0 to 511, as said below
- weights: bfloat16 [32768, 4], P(('lat', 'lon')), may hold values from 0.099609375 to 1
- obs_proj: bfloat16 [256, 512], replicated, may hold values from -0.375 to 0.375
- depth_w: float32 [4, 7, 7, 512], replicated, may hold values from -1.5 to 1.5
- point_w: bfloat16 [4, 512, 512], replicated, may hold values from -0.25 to 0.25
- gains: float32 [4, 512], replicated, may hold values from 0.5 to 2
Outputs:
- encoded: bfloat16 [64, 256, 512], P('lat', 'lon')
Inputs may be any that keep to these rules, and one draw needn't show every extreme that they name: `destination`: each device's 1024 rows name one tile at most 64 times. footprint[i, k] = (s_i + k * 33) mod 512 for a start cell s_i, so the 4 cells of one observation are distinct.
All inputs are finite; a program needn't handle non-finite values.
Results may differ from a plain program's by a relative error of at most 0.0085.
Values may be sent and summed in bfloat16 or wider, within the bound.
No kernel may reach another device: no remote copies, remote signals or barrier semaphores. Data moves between devices by JAX's collectives and lax.ppermute only.
A program may use at most 64 MiB of HBM per device.

v0:
```python
import functools

import jax
import jax.numpy as jnp
from jax import lax
from jax.experimental import pallas as pl
from jax.experimental.pallas import tpu as pltpu
from jax.sharding import PartitionSpec as P

LANES = 128
META = 8
TAPS = 7
HALO = 3
SHIFT = 2 * HALO
EDGE = 8
SUBLANES = 8
TILE = 16
SPARE = 4
VMEM_LIMIT = 24 * 1024 * 1024
BF16 = jnp.bfloat16
F32 = jnp.float32


def pack_kernel(cap, cols, dest_hbm, foot_hbm, weights_hbm, obs_hbm, send_ref, dest_ref, foot_ref, weights_ref, obs_ref, sems):
    copies = [
        pltpu.make_async_copy(source, target, sems.at[k])
        for k, (source, target) in enumerate(
            (
                (dest_hbm, dest_ref),
                (obs_hbm, obs_ref),
                (foot_hbm, foot_ref),
                (weights_hbm, weights_ref),
            )
        )
    ]
    for copy in copies:
        copy.start()
    devices = send_ref.shape[0]
    obs_rows = obs_ref.shape[0]
    per = LANES // cap
    upper = lax.broadcasted_iota(jnp.int32, (LANES, LANES), 0) <= lax.broadcasted_iota(
        jnp.int32, (LANES, LANES), 1
    )
    upper = jnp.where(upper, 1.0, 0.0).astype(BF16)
    ids = lax.broadcasted_iota(jnp.int32, (devices, obs_rows), 0)
    copies[0].wait()
    member = jnp.where(ids == dest_ref[...], 1.0, 0.0)
    seen = jnp.zeros((devices, 1), F32)
    ranks = []
    for first in range(0, obs_rows, LANES):
        part = member[:, first : first + LANES]
        count = jnp.dot(part.astype(BF16), upper, preferred_element_type=F32) + seen
        ranks.append(jnp.sum((count - 1.0) * part, axis=0, keepdims=True))
        seen = count[:, LANES - 1 :]
    rank = jnp.concatenate(ranks, axis=1).astype(jnp.int32)
    slot = lax.broadcasted_iota(jnp.int32, (cap, obs_rows), 0)
    ranked = jnp.where(slot == rank, 1.0, 0.0).astype(BF16).reshape(cap // TILE, TILE, obs_rows)
    for copy in copies[1:]:
        copy.wait()
    start = foot_ref[0:1, :]
    meta = jnp.concatenate(
        [
            lax.div(start, cols).astype(F32),
            lax.rem(start, cols).astype(F32),
            weights_ref[...].astype(F32),
            jnp.zeros((META - 2 - weights_ref.shape[0], obs_rows), F32),
        ],
        axis=0,
    ).astype(BF16)
    obs = obs_ref[...]
    lane = lax.broadcasted_iota(jnp.int32, (META, LANES), 1)
    count = min(512, devices * cap) // cap
    for first in range(0, devices, count):
        parts = []
        for d in range(first, first + count):
            mine = jnp.broadcast_to(member[d : d + 1], (TILE, obs_rows)).astype(BF16)
            parts.append((ranked * mine[None]).reshape(cap, obs_rows))
        chosen = jnp.concatenate(parts, axis=0)
        feats = jnp.dot(chosen, obs, preferred_element_type=F32).astype(BF16)
        placed = lax.dot_general(
            meta, chosen, (((1,), (1,)), ((), ())), preferred_element_type=F32
        )
        for half in range(feats.shape[1] // LANES):
            piece = feats[:, half * LANES : (half + 1) * LANES].reshape(count, cap, LANES)
            send_ref[first : first + count, half * cap : (half + 1) * cap, :] = piece
        base = send_ref.shape[1] - META
        for chunk in range(count // per):
            values = placed[:, chunk * LANES : (chunk + 1) * LANES]
            turned = [values] + [pltpu.roll(values, k * cap, 1) for k in range(1, per)]
            for own in range(per):
                wide = turned[0]
                for group in range(per):
                    wide = jnp.where(lane // cap == group, turned[(group - own) % per], wide)
                send_ref[first + chunk * per + own, base:, :] = wide.astype(BF16)


def assim_kernel(cap, step, got_ref, proj_ref, back_ref, state_ref, lat_ref, lon_ref, corner_ref):
    devices, depth, _ = got_ref.shape
    rows, cols, chans = back_ref.shape
    cells = rows * cols
    feats = proj_ref.shape[0]
    per = LANES // cap
    halves = feats // LANES
    lane = lax.broadcasted_iota(jnp.int32, (META, LANES), 1)
    cell = lax.broadcasted_iota(jnp.int32, (cells, LANES), 0)
    total = jnp.zeros((cells, feats), F32)
    for pair in range(0, devices // per, 2):
        maps = []
        blocks = []
        for chunk in (pair, pair + 1):
            meta = got_ref[chunk * per, depth - META :, :].astype(F32)
            for group in range(1, per):
                other = got_ref[chunk * per + group, depth - META :, :].astype(F32)
                meta = jnp.where(lane // cap == group, other, meta)
            start = (meta[0:1] * cols + meta[1:2]).astype(jnp.int32)
            away = cell - start
            away = jnp.where(away < 0, away + cells, away)
            amount = jnp.zeros((cells, LANES), F32)
            for entry in range(4):
                amount = jnp.where(away == entry * step, meta[2 + entry : 3 + entry], amount)
            maps.append(amount.astype(BF16))
            block = got_ref[chunk * per : (chunk + 1) * per]
            blocks.append(
                jnp.concatenate(
                    [
                        block[:, half * cap : (half + 1) * cap, :].reshape(LANES, LANES)
                        for half in range(halves)
                    ],
                    axis=1,
                )
            )
        total = total + jnp.dot(
            jnp.concatenate(maps, axis=1),
            jnp.concatenate(blocks, axis=0),
            preferred_element_type=F32,
        )
    assim = jnp.dot(total.astype(BF16), proj_ref[...], preferred_element_type=F32)
    state = back_ref[...].astype(F32) + assim.reshape(rows, cols, chans)
    state = state.astype(BF16)
    state_ref[...] = state
    lat_ref[...] = state[rows - SHIFT :]
    lon_ref[...] = state[:, cols - EDGE :, :]
    corner_ref[...] = state[rows - SHIFT :, cols - EDGE :, :]


def gelu(x):
    inner = x * (0.7978845608028654 + 0.035677408136300125 * (x * x))
    half = 0.5 * x
    return half + half * jnp.tanh(inner)


def layer_kernel(
    shrink,
    own_ref,
    lat_in,
    lon_in,
    corner_in,
    taps_ref,
    mix_ref,
    state_ref,
    lat_ref,
    lon_ref,
    corner_ref,
    wide_ref,
    taps_in,
    spread_ref,
    out_ref,
):
    chans = mix_ref.shape[0]
    groups = chans // LANES
    cols = own_ref.shape[1]
    phases = cols // SUBLANES
    place = lax.axis_index("lat")
    last = place == lax.axis_size("lat") - 1
    first = place == 0
    rows = state_ref.shape[0] if shrink else own_ref.shape[0]

    def put(row, start, value):
        for g in range(groups):
            wide_ref[g, row, start : start + value.shape[0], :] = value[
                :, g * LANES : (g + 1) * LANES
            ]

    if shrink:
        base = 0

        @pl.loop(0, rows, unroll=2)
        def _(y):
            put(y, 0, own_ref[y].astype(F32))
            put(y, cols, lon_in[y].astype(F32))

        for k in range(SHIFT):
            main = lat_in[k].astype(F32)
            side = corner_in[k].astype(F32)
            if k < HALO:
                main = jnp.where(last, own_ref[rows + k].astype(F32), main)
                side = jnp.where(last, lon_in[rows + k].astype(F32), side)
            else:
                main = jnp.where(last, 0.0, main)
                side = jnp.where(last, 0.0, side)
            put(rows + k, 0, main)
            put(rows + k, cols, side)
    else:
        base = EDGE - SHIFT

        @pl.loop(0, SHIFT, unroll=2)
        def _(y):
            put(y, 0, jnp.where(first, 0.0, corner_in[y].astype(F32)))
            put(y, EDGE, jnp.where(first, 0.0, lat_in[y].astype(F32)))

        @pl.loop(0, rows, unroll=2)
        def _(y):
            put(y + SHIFT, 0, lon_in[y].astype(F32))
            put(y + SHIFT, EDGE, own_ref[y].astype(F32))

    ones = jnp.ones((chans, LANES), BF16)

    def stage(top, high):
        @pl.loop(0, high + TAPS - 1, unroll=2)
        def _(y):
            for g in range(groups):
                for r in range(phases + TAPS - 1):
                    both = [
                        wide_ref[g, top + y + h, pl.ds(base + r, SUBLANES, stride=phases), :]
                        for h in (0, high)
                    ]
                    taps_in[g, r, y] = jnp.concatenate(both, axis=0).astype(BF16)

        def depthwise(p):
            for g in range(groups):
                total = None
                for b in range(TAPS):
                    seen = taps_in[g, p + b, 0 : high + TAPS - 1]
                    part = None
                    for a in range(TAPS):
                        term = seen[a : a + high] * taps_ref[g, a * TAPS + b]
                        part = term if part is None else part + term
                    part = part.astype(F32)
                    total = part if total is None else total + part
                spread_ref[p % 2, 0:high, :, g * LANES : (g + 1) * LANES] = total.astype(BF16)

        def finish(p):
            spread = spread_ref[p % 2, 0:high].reshape(high * TILE, chans)
            power = jnp.dot(spread * spread, ones, preferred_element_type=F32)
            scale = lax.rsqrt(power * (1.0 / chans) + 1e-05)
            mixed = jnp.dot(spread, mix_ref[...], preferred_element_type=F32)
            for g in range(groups):
                moved = gelu(mixed[:, g * LANES : (g + 1) * LANES] * scale)
                moved = moved.reshape(high, TILE, LANES)
                center = taps_in[g, p + HALO, HALO : HALO + high].astype(F32)
                fresh = center + moved
                for k in range(high):
                    for h in range(2):
                        out_ref[g, top + h * high + k, pl.ds(p, SUBLANES, stride=phases), :] = (
                            fresh[k, h * SUBLANES : (h + 1) * SUBLANES]
                        )

        depthwise(0)

        @pl.loop(1, phases)
        def _(p):
            finish(p - 1)
            depthwise(p)

        finish(phases - 1)

    stage(0, rows // 2)

    def row_of(y):
        return jnp.concatenate([out_ref[g, y] for g in range(groups)], axis=1)

    if shrink:
        edge = slice(cols - EDGE, cols)

        @pl.loop(0, rows, unroll=2)
        def _(y):
            value = row_of(y)
            state_ref[y] = value.astype(BF16)
            lon_ref[y] = value[edge].astype(BF16)

        for k in range(SHIFT):
            value = row_of(rows - SHIFT + k)
            lat_ref[k] = value.astype(BF16)
            corner_ref[k] = value[edge].astype(BF16)
    else:

        @pl.when(last)
        def _():
            wide_ref[:, rows + SHIFT :] = jnp.zeros(
                (groups, SPARE, wide_ref.shape[2], LANES), F32
            )
            stage(rows, SPARE // 2)

        def masked(y):
            return jnp.where(jnp.logical_and(first, y < HALO), 0.0, row_of(y))

        @pl.loop(0, rows, unroll=2)
        def _(y):
            value = masked(y)
            state_ref[y] = value.astype(BF16)
            lon_ref[y] = value[:EDGE].astype(BF16)

        for k in range(HALO):
            value = row_of(rows + k)
            state_ref[rows + k] = value.astype(BF16)
            lon_ref[rows + k] = value[:EDGE].astype(BF16)

        for k in range(SHIFT):
            value = masked(k)
            lat_ref[k] = value.astype(BF16)
            corner_ref[k] = value[:EDGE].astype(BF16)


def edges(rows, cols, chans):
    return (
        jax.ShapeDtypeStruct((rows, cols, chans), BF16),
        jax.ShapeDtypeStruct((SHIFT, cols, chans), BF16),
        jax.ShapeDtypeStruct((rows, EDGE, chans), BF16),
        jax.ShapeDtypeStruct((SHIFT, EDGE, chans), BF16),
    )


def call(kernel, out_shape, inputs, scratch=(), space=pltpu.VMEM):
    whole = pl.BlockSpec(memory_space=pltpu.VMEM)
    single = isinstance(out_shape, jax.ShapeDtypeStruct)
    return pl.pallas_call(
        kernel,
        out_shape=out_shape,
        in_specs=[pl.BlockSpec(memory_space=space)] * len(inputs),
        out_specs=whole if single else [whole] * len(out_shape),
        scratch_shapes=list(scratch),
        compiler_params=pltpu.CompilerParams(vmem_limit_bytes=VMEM_LIMIT),
    )(*inputs)


def layer(state, halo, taps, mix, shrink):
    extended, cols, chans = state.shape
    rows = extended - HALO if shrink else extended
    groups = chans // LANES
    phases = cols // SUBLANES
    height = rows if shrink else rows + HALO
    spare = 0 if shrink else SPARE
    scratch = (
        pltpu.VMEM((groups, rows + SHIFT + spare, cols + EDGE, LANES), F32),
        pltpu.VMEM((groups, phases + TAPS - 1, rows // 2 + TAPS - 1, TILE, LANES), BF16),
        pltpu.VMEM((2, rows // 2, TILE, chans), BF16),
        pltpu.VMEM((groups, rows + spare, cols, LANES), F32),
    )
    return call(
        functools.partial(layer_kernel, shrink),
        edges(height, cols, chans),
        (state, *halo, taps, mix),
        scratch,
    )


def exchange(pieces, forward):
    lat, lon, corner = pieces
    count_lat = lax.axis_size("lat")
    count_lon = lax.axis_size("lon")
    along = [(i, (i + 1) % count_lat) for i in range(count_lat)]
    around = [(j, (j + 1) % count_lon) for j in range(count_lon)]
    across = [
        (i * count_lon + j, ni * count_lon + nj) for i, ni in along for j, nj in around
    ]
    if not forward:
        along, around, across = ([(t, s) for s, t in p] for p in (along, around, across))
    return (
        lax.ppermute(lat, "lat", along),
        lax.ppermute(lon, "lon", around),
        lax.ppermute(corner, ("lat", "lon"), across),
    )


def body(
    background, observations, destination, footprint, weights, obs_proj, depth_w, point_w, gains
):
    rows, cols, chans = background.shape
    devices = lax.axis_size("lat") * lax.axis_size("lon")
    obs_rows, feats = observations.shape
    cap = 2 * obs_rows // devices
    depth = cap * (feats // LANES) + META
    foot_count = footprint.shape[1]
    send = call(
        functools.partial(pack_kernel, cap, cols),
        jax.ShapeDtypeStruct((devices, depth, LANES), BF16),
        (destination.T, footprint.T, weights.T, observations),
        (
            pltpu.VMEM((1, obs_rows), jnp.int32),
            pltpu.VMEM((foot_count, obs_rows), jnp.int32),
            pltpu.VMEM((foot_count, obs_rows), BF16),
            pltpu.VMEM((obs_rows, feats), BF16),
            pltpu.SemaphoreType.DMA((4,)),
        ),
        pltpu.HBM,
    )
    got = lax.all_to_all(send, ("lat", "lon"), split_axis=0, concat_axis=0, tiled=True)
    layers = depth_w.shape[0]
    groups = chans // LANES
    taps = depth_w.astype(BF16).reshape(layers, TAPS * TAPS, groups, LANES).transpose(0, 2, 1, 3)
    taps = [
        jnp.broadcast_to(taps[n][:, :, None], (groups, TAPS * TAPS, TILE, LANES))
        for n in range(layers)
    ]
    mix = [(gains[n][:, None] * point_w[n].astype(F32)).astype(BF16) for n in range(layers)]
    got, taps, mix = lax.optimization_barrier((got, taps, mix))
    state, *pieces = call(
        functools.partial(assim_kernel, cap, cols + 1),
        edges(rows, cols, chans),
        (got, obs_proj, background),
    )
    for n in range(layers):
        shrink = n % 2 == 1
        halo = exchange(pieces, not shrink)
        state, *pieces = layer(state, halo, taps[n], mix[n], shrink)
    return state


def solution(mesh):
    placed = (
        P("lat", "lon", None),
        P(("lat", "lon"), None),
        P(("lat", "lon"), None),
        P(("lat", "lon"), None),
        P(("lat", "lon"), None),
        P(),
        P(),
        P(),
        P(),
    )
    return jax.shard_map(
        body, mesh=mesh, in_specs=placed, out_specs=P("lat", "lon", None), check_vma=False
    )
```

profile of v0, /device:TPU:0, one launch (start us, length us, event | category | flops | bytes accessed | tf_op | source)
XLA Modules:
  0.0 111.1 jit_solution(17075904456018065699)
XLA Ops:
  0.0 1.0 copy-done
  1.0 0.7 copy-done.3
  3.1 4.1 %shard_map.91 = bf16[32,136,128]{2,1,0:T(8,128)(2,1)} custom-call(s32[1,1024]{1,0:T(1,128)S(1)} %bitcast.34, s32[4,1024]{1,0:T(4,128)S(1)} %bitcast.32, bf16[4,1024]{1,0:T(4,128)(2,1)S(1)} %bitcast.33, bf16[1024,256]{1,0:T(8,128)(2,1)S(1)} %copy-done), custom_call_target="tpu_custom_call" | custom-call | tf_op jit(solution)/shard_map/pallas_call | solution.py:326
  7.3 7.3 %all-to-all-start = ((bf16[32,136,128]{2,1,0:T(8,128)(2,1)}), bf16[32,136,128]{2,1,0:T(8,128)(2,1)S(1)}, u32[]{:S(2)}, u32[]{:S(2)}) async-start(bf16[32,136,128]{2,1,0:T(8,128)(2,1)} %shard_map.91), calls=%async_computation | async-start | bytes 2228224 | tf_op jit(solution)/shard_map/all_to_all | solution.py:397
  15.5 2.0 %fusion = (bf16[512,512]{1,0:T(8,128)(2,1)S(1)}, bf16[512,512]{1,0:T(8,128)(2,1)S(1)}, bf16[512,512]{1,0:T(8,128)(2,1)S(1)}, bf16[512,512]{1,0:T(8,128)(2,1)S(1)}) fusion(bf16[4,512,512]{2,1,0:T(8,128)(2,1)} %param.16, f32[512]{0:T(512)S(1)} %bitcast.36, f32[512]{0:T(512)S(1)} %bitcast.37, f32[512]{0:T(512)S(1)} %bitcast.38, f32[512]{0:T(512)S(1)} %bitcast.39), kind=kLoop, calls=%fused_computation.1 | loop fusion | flops 3145728 | bytes 4202496 | tf_op jit(solution)/shard_map/convert_element_type | solution.py:405
  17.5 26.1 %all-to-all-done.got_ref = bf16[32,136,128]{2,1,0:T(8,128)(2,1)S(1)} async-done(((bf16[32,136,128]{2,1,0:T(8,128)(2,1)}), bf16[32,136,128]{2,1,0:T(8,128)(2,1)S(1)}, u32[]{:S(2)}, u32[]{:S(2)}) %all-to-all-start) | async-done | bytes 1114144 | tf_op jit(solution)/shard_map/all_to_all | solution.py:397
  43.6 1.0 broadcast_in_dim.35.taps_ref
  44.6 0.9 broadcast_in_dim.33.taps_ref
  45.5 0.9 broadcast_in_dim.31.taps_ref
  46.6 2.2 %shard_map.92 = (bf16[16,32,512]{2,1,0:T(8,128)(2,1)S(1)}, bf16[6,32,512]{2,1,0:T(8,128)(2,1)S(1)}, bf16[16,8,512]{2,1,0:T(8,128)(2,1)S(1)}, bf16[6,8,512]{2,1,0:T(8,128)(2,1)S(1)}) custom-call(bf16[32,136,128]{2,1,0:T(8,128)(2,1)S(1)} %all-to-all-done.got_ref, bf16[256,512]{1,0:T(8,128)(2,1)S(1)} %copy-done.2, bf16[16,32,512]{2,1,0:T(8,128)(2,1)S(1)} %copy-done.1), custom_call_target="tpu_custom_call" | custom-call | tf_op jit(solution)/shard_map/pallas_call | solution.py:326
  49.4 1.1 collective-permute-start.2
  50.5 7.4 %collective-permute-done.2.corner_in = bf16[6,8,512]{2,1,0:T(8,128)(2,1)S(1)} collective-permute-done((bf16[6,8,512]{2,1,0:T(8,128)(2,1)S(1)}, bf16[6,8,512]{2,1,0:T(8,128)(2,1)S(1)}, u32[]{:S(2)}, u32[]{:S(2)}) %collective-permute-start.2) | collective-permute-done | bytes 49184 | tf_op jit(solution)/shard_map/ppermute | solution.py:371
  57.9 6.8 %shard_map.93 = (bf16[19,32,512]{2,1,0:T(8,128)(2,1)S(1)}, bf16[6,32,512]{2,1,0:T(8,128)(2,1)S(1)}, bf16[19,8,512]{2,1,0:T(8,128)(2,1)S(1)}, bf16[6,8,512]{2,1,0:T(8,128)(2,1)S(1)}) custom-call(bf16[16,32,512]{2,1,0:T(8,128)(2,1)S(1)} %get-tuple-element.32.own_ref, bf16[6,32,512]{2,1,0:T(8,128)(2,1)S(1)} %collective-permute-done.lat_in, ...), custom_call_target="tpu_custom_call" | custom-call | tf_op jit(solution)/shard_map/pallas_call | solution.py:326
  64.8 2.3 %collective-permute-start.3 = (bf16[6,32,512]{2,1,0:T(8,128)(2,1)S(1)}, bf16[6,32,512]{2,1,0:T(8,128)(2,1)S(1)}, u32[]{:S(2)}, u32[]{:S(2)}) collective-permute-start(bf16[6,32,512]{2,1,0:T(8,128)(2,1)S(1)} %get-tuple-element.39), channel_id=1, source_target_pairs={{8,0},{16,8},{24,16},{0,24},{9,1},{17,9},{25,17},{1,25},{10,2},{18... | collective-permute-start | bytes 589832 | tf_op jit(solution)/shard_map/ppermute | solution.py:369
  67.7 3.5 %collective-permute-done.5.corner_in = bf16[6,8,512]{2,1,0:T(8,128)(2,1)S(1)} collective-permute-done((bf16[6,8,512]{2,1,0:T(8,128)(2,1)S(1)}, bf16[6,8,512]{2,1,0:T(8,128)(2,1)S(1)}, u32[]{:S(2)}, u32[]{:S(2)}) %collective-permute-start.5) | collective-permute-done | bytes 49184 | tf_op jit(solution)/shard_map/ppermute | solution.py:371
  71.6 6.8 %shard_map.94 = (bf16[16,32,512]{2,1,0:T(8,128)(2,1)S(1)}, bf16[6,32,512]{2,1,0:T(8,128)(2,1)S(1)}, bf16[16,8,512]{2,1,0:T(8,128)(2,1)S(1)}, bf16[6,8,512]{2,1,0:T(8,128)(2,1)S(1)}) custom-call(bf16[19,32,512]{2,1,0:T(8,128)(2,1)S(1)} %get-tuple-element.38.own_ref, bf16[6,32,512]{2,1,0:T(8,128)(2,1)S(1)} %collective-permute-done.3.lat_in, ...), custom_call_target="tpu_custom_call" | custom-call | tf_op jit(solution)/shard_map/pallas_call | solution.py:326
  78.4 1.5 %collective-permute-start.6 = (bf16[6,32,512]{2,1,0:T(8,128)(2,1)S(1)}, bf16[6,32,512]{2,1,0:T(8,128)(2,1)S(1)}, u32[]{:S(2)}, u32[]{:S(2)}) collective-permute-start(bf16[6,32,512]{2,1,0:T(8,128)(2,1)S(1)} %get-tuple-element.45), channel_id=1, source_target_pairs={{0,8},{8,16},{16,24},{24,0},{1,9},{9,17},{17,25},{25,1},{2,10},{10... | collective-permute-start | bytes 589832 | tf_op jit(solution)/shard_map/ppermute | solution.py:369
  79.9 0.9 collective-permute-start.8
  80.8 7.2 %collective-permute-done.8.corner_in = bf16[6,8,512]{2,1,0:T(8,128)(2,1)S(1)} collective-permute-done((bf16[6,8,512]{2,1,0:T(8,128)(2,1)S(1)}, bf16[6,8,512]{2,1,0:T(8,128)(2,1)S(1)}, u32[]{:S(2)}, u32[]{:S(2)}) %collective-permute-start.8) | collective-permute-done | bytes 49184 | tf_op jit(solution)/shard_map/ppermute | solution.py:371
  88.0 6.8 %shard_map.95 = (bf16[19,32,512]{2,1,0:T(8,128)(2,1)S(1)}, bf16[6,32,512]{2,1,0:T(8,128)(2,1)S(1)}, bf16[19,8,512]{2,1,0:T(8,128)(2,1)S(1)}, bf16[6,8,512]{2,1,0:T(8,128)(2,1)S(1)}) custom-call(bf16[16,32,512]{2,1,0:T(8,128)(2,1)S(1)} %get-tuple-element.44.own_ref, bf16[6,32,512]{2,1,0:T(8,128)(2,1)S(1)} %collective-permute-done.6.lat_in, ...), custom_call_target="tpu_custom_call" | custom-call | tf_op jit(solution)/shard_map/pallas_call | solution.py:326
  94.9 4.2 %collective-permute-start.9 = (bf16[6,32,512]{2,1,0:T(8,128)(2,1)S(1)}, bf16[6,32,512]{2,1,0:T(8,128)(2,1)S(1)}, u32[]{:S(2)}, u32[]{:S(2)}) collective-permute-start(bf16[6,32,512]{2,1,0:T(8,128)(2,1)S(1)} %get-tuple-element.51), channel_id=1, source_target_pairs={{8,0},{16,8},{24,16},{0,24},{9,1},{17,9},{25,17},{1,25},{10,2},{18... | collective-permute-start | bytes 589832 | tf_op jit(solution)/shard_map/ppermute | solution.py:369
  99.0 0.9 collective-permute-start.10
  99.9 3.5 %collective-permute-done.11.corner_in = bf16[6,8,512]{2,1,0:T(8,128)(2,1)S(1)} collective-permute-done((bf16[6,8,512]{2,1,0:T(8,128)(2,1)S(1)}, bf16[6,8,512]{2,1,0:T(8,128)(2,1)S(1)}, u32[]{:S(2)}, u32[]{:S(2)}) %collective-permute-start.11) | collective-permute-done | bytes 49184 | tf_op jit(solution)/shard_map/ppermute | solution.py:371
  103.4 7.6 %shard_map.96 = (bf16[16,32,512]{2,1,0:T(8,128)(2,1)}, bf16[6,32,512]{2,1,0:T(8,128)(2,1)}, bf16[16,8,512]{2,1,0:T(8,128)(2,1)}, bf16[6,8,512]{2,1,0:T(8,128)(2,1)}) custom-call(bf16[19,32,512]{2,1,0:T(8,128)(2,1)S(1)} %get-tuple-element.50.own_ref, bf16[6,32,512]{2,1,0:T(8,128)(2,1)S(1)} %collective-permute-done.9.lat_in, ...), custom_call_target="tpu_custom_call" | custom-call | tf_op jit(solution)/shard_map/pallas_call | solution.py:326
  (34 shorter events, 4.1 us)
Async XLA Ops:
  0.0 1.0 copy-start
  1.0 0.7 copy-start.3
  1.8 0.7 copy-start.4
  2.5 0.7 copy-start.5
  3.1 11.5 %copy-start.6 = (f32[4,7,7,512]{3,0,2,1:T(4,128)S(1)}, f32[4,7,7,512]{3,0,2,1:T(4,128)}, u32[]{:S(2)}) copy-start(f32[4,7,7,512]{3,0,2,1:T(4,128)} %param.15) | copy-start | bytes 1204228
  7.3 7.6 %copy-start.7 = (f32[4,512]{1,0:T(4,128)S(1)}, f32[4,512]{1,0:T(4,128)}, u32[]{:S(2)}) copy-start(f32[4,512]{1,0:T(4,128)} %param.17) | copy-start | bytes 24580
  7.3 36.3 %all-to-all-start = ((bf16[32,136,128]{2,1,0:T(8,128)(2,1)}), bf16[32,136,128]{2,1,0:T(8,128)(2,1)S(1)}, u32[]{:S(2)}, u32[]{:S(2)}) async-start(bf16[32,136,128]{2,1,0:T(8,128)(2,1)} %shard_map.91), calls=%async_computation | async-start | bytes 2228224 | tf_op jit(solution)/shard_map/all_to_all | solution.py:397
  17.5 29.0 %copy-start.2 = (bf16[256,512]{1,0:T(8,128)(2,1)S(1)}, bf16[256,512]{1,0:T(8,128)(2,1)}, u32[]{:S(2)}) copy-start(bf16[256,512]{1,0:T(8,128)(2,1)} %proj_ref.1) | copy-start | bytes 786436
  43.6 3.0 %copy-start.1 = (bf16[16,32,512]{2,1,0:T(8,128)(2,1)S(1)}, bf16[16,32,512]{2,1,0:T(8,128)(2,1)}, u32[]{:S(2)}) copy-start(bf16[16,32,512]{2,1,0:T(8,128)(2,1)} %back_ref.1) | copy-start | bytes 1572868
  48.8 9.1 %collective-permute-start = (bf16[6,32,512]{2,1,0:T(8,128)(2,1)S(1)}, bf16[6,32,512]{2,1,0:T(8,128)(2,1)S(1)}, u32[]{:S(2)}, u32[]{:S(2)}) collective-permute-start(bf16[6,32,512]{2,1,0:T(8,128)(2,1)S(1)} %get-tuple-element.33), channel_id=1, source_target_pairs={{0,8},{8,16},{16,24},{24,0},{1,9},{9,17},{17,25},{25,1},{2,10},{10... | collective-permute-start | bytes 589832 | tf_op jit(solution)/shard_map/ppermute | solution.py:369
  48.9 9.1 %collective-permute-start.1 = (bf16[16,8,512]{2,1,0:T(8,128)(2,1)S(1)}, bf16[16,8,512]{2,1,0:T(8,128)(2,1)S(1)}, u32[]{:S(2)}, u32[]{:S(2)}) collective-permute-start(bf16[16,8,512]{2,1,0:T(8,128)(2,1)S(1)} %get-tuple-element.34), channel_id=1, source_target_pairs={{0,1},{1,2},{2,3},{3,4},{4,5},{5,6},{6,7},{7,0},{8,9},{9,10},{10,1... | collective-permute-start | bytes 393224 | tf_op jit(solution)/shard_map/ppermute | solution.py:370
  49.4 8.5 %collective-permute-start.2 = (bf16[6,8,512]{2,1,0:T(8,128)(2,1)S(1)}, bf16[6,8,512]{2,1,0:T(8,128)(2,1)S(1)}, u32[]{:S(2)}, u32[]{:S(2)}) collective-permute-start(bf16[6,8,512]{2,1,0:T(8,128)(2,1)S(1)} %get-tuple-element.35), channel_id=1, source_target_pairs={{0,9},{1,10},{2,11},{3,12},{4,13},{5,14},{6,15},{7,8},{8,17},{9,18... | collective-permute-start | bytes 147464 | tf_op jit(solution)/shard_map/ppermute | solution.py:371
  64.8 6.8 %collective-permute-start.3 = (bf16[6,32,512]{2,1,0:T(8,128)(2,1)S(1)}, bf16[6,32,512]{2,1,0:T(8,128)(2,1)S(1)}, u32[]{:S(2)}, u32[]{:S(2)}) collective-permute-start(bf16[6,32,512]{2,1,0:T(8,128)(2,1)S(1)} %get-tuple-element.39), channel_id=1, source_target_pairs={{8,0},{16,8},{24,16},{0,24},{9,1},{17,9},{25,17},{1,25},{10,2},{18... | collective-permute-start | bytes 589832 | tf_op jit(solution)/shard_map/ppermute | solution.py:369
  67.1 4.1 %collective-permute-start.4 = (bf16[19,8,512]{2,1,0:T(8,128)(2,1)S(1)}, bf16[19,8,512]{2,1,0:T(8,128)(2,1)S(1)}, u32[]{:S(2)}, u32[]{:S(2)}) collective-permute-start(bf16[19,8,512]{2,1,0:T(8,128)(2,1)S(1)} %get-tuple-element.40), channel_id=1, source_target_pairs={{1,0},{2,1},{3,2},{4,3},{5,4},{6,5},{7,6},{0,7},{9,8},{10,9},{11,1... | collective-permute-start | bytes 466952 | tf_op jit(solution)/shard_map/ppermute | solution.py:370
  67.6 3.5 %collective-permute-start.5 = (bf16[6,8,512]{2,1,0:T(8,128)(2,1)S(1)}, bf16[6,8,512]{2,1,0:T(8,128)(2,1)S(1)}, u32[]{:S(2)}, u32[]{:S(2)}) collective-permute-start(bf16[6,8,512]{2,1,0:T(8,128)(2,1)S(1)} %get-tuple-element.41), channel_id=1, source_target_pairs={{9,0},{10,1},{11,2},{12,3},{13,4},{14,5},{15,6},{8,7},{17,8},{18,9... | collective-permute-start | bytes 147464 | tf_op jit(solution)/shard_map/ppermute | solution.py:371
  78.4 9.7 %collective-permute-start.6 = (bf16[6,32,512]{2,1,0:T(8,128)(2,1)S(1)}, bf16[6,32,512]{2,1,0:T(8,128)(2,1)S(1)}, u32[]{:S(2)}, u32[]{:S(2)}) collective-permute-start(bf16[6,32,512]{2,1,0:T(8,128)(2,1)S(1)} %get-tuple-element.45), channel_id=1, source_target_pairs={{0,8},{8,16},{16,24},{24,0},{1,9},{9,17},{17,25},{25,1},{2,10},{10... | collective-permute-start | bytes 589832 | tf_op jit(solution)/shard_map/ppermute | solution.py:369
  79.9 8.1 %collective-permute-start.7 = (bf16[16,8,512]{2,1,0:T(8,128)(2,1)S(1)}, bf16[16,8,512]{2,1,0:T(8,128)(2,1)S(1)}, u32[]{:S(2)}, u32[]{:S(2)}) collective-permute-start(bf16[16,8,512]{2,1,0:T(8,128)(2,1)S(1)} %get-tuple-element.46), channel_id=1, source_target_pairs={{0,1},{1,2},{2,3},{3,4},{4,5},{5,6},{6,7},{7,0},{8,9},{9,10},{10,1... | collective-permute-start | bytes 393224 | tf_op jit(solution)/shard_map/ppermute | solution.py:370
  79.9 8.1 %collective-permute-start.8 = (bf16[6,8,512]{2,1,0:T(8,128)(2,1)S(1)}, bf16[6,8,512]{2,1,0:T(8,128)(2,1)S(1)}, u32[]{:S(2)}, u32[]{:S(2)}) collective-permute-start(bf16[6,8,512]{2,1,0:T(8,128)(2,1)S(1)} %get-tuple-element.47), channel_id=1, source_target_pairs={{0,9},{1,10},{2,11},{3,12},{4,13},{5,14},{6,15},{7,8},{8,17},{9,18... | collective-permute-start | bytes 147464 | tf_op jit(solution)/shard_map/ppermute | solution.py:371
  94.9 8.6 %collective-permute-start.9 = (bf16[6,32,512]{2,1,0:T(8,128)(2,1)S(1)}, bf16[6,32,512]{2,1,0:T(8,128)(2,1)S(1)}, u32[]{:S(2)}, u32[]{:S(2)}) collective-permute-start(bf16[6,32,512]{2,1,0:T(8,128)(2,1)S(1)} %get-tuple-element.51), channel_id=1, source_target_pairs={{8,0},{16,8},{24,16},{0,24},{9,1},{17,9},{25,17},{1,25},{10,2},{18... | collective-permute-start | bytes 589832 | tf_op jit(solution)/shard_map/ppermute | solution.py:369
  99.0 4.4 %collective-permute-start.10 = (bf16[19,8,512]{2,1,0:T(8,128)(2,1)S(1)}, bf16[19,8,512]{2,1,0:T(8,128)(2,1)S(1)}, u32[]{:S(2)}, u32[]{:S(2)}) collective-permute-start(bf16[19,8,512]{2,1,0:T(8,128)(2,1)S(1)} %get-tuple-element.52), channel_id=1, source_target_pairs={{1,0},{2,1},{3,2},{4,3},{5,4},{6,5},{7,6},{0,7},{9,8},{10,9},{11,1... | collective-permute-start | bytes 466952 | tf_op jit(solution)/shard_map/ppermute | solution.py:370
  99.9 3.5 %collective-permute-start.11 = (bf16[6,8,512]{2,1,0:T(8,128)(2,1)S(1)}, bf16[6,8,512]{2,1,0:T(8,128)(2,1)S(1)}, u32[]{:S(2)}, u32[]{:S(2)}) collective-permute-start(bf16[6,8,512]{2,1,0:T(8,128)(2,1)S(1)} %get-tuple-element.53), channel_id=1, source_target_pairs={{9,0},{10,1},{11,2},{12,3},{13,4},{14,5},{15,6},{8,7},{17,8},{18,9... | collective-permute-start | bytes 147464 | tf_op jit(solution)/shard_map/ppermute | solution.py:371
where the time goes:
time: 112 us; the launch traced here: 111 us
  waiting for transfers between devices  48.2 us (43%)
  Pallas kernels  34.4 us (31%)
  starting transfers between devices  19.4 us (17%)
  local copies, waits for them, and re-layouts  6.91 us (6%)
  other arithmetic  2.05 us (2%)
    pallas_call x6, Pallas kernels, call(): pl.pallas_call(kernel, out_shape=out_shape, in_specs=[pl.BlockSpec(memory...  34.4 us
    all_to_all x1, waiting for transfers between devices, body(): lax.all_to_all(send, ('lat', 'lon'), split_axis=0, concat_axis=0, tiled=T...  26.1 us
    ppermute x4, waiting for transfers between devices, exchange(): lax.ppermute(corner, ('lat', 'lon'), across)  21.7 us
    ppermute x4, starting transfers between devices, exchange(): lax.ppermute(lat, 'lat', along)  8.05 us
    all_to_all x1, starting transfers between devices, body(): lax.all_to_all(send, ('lat', 'lon'), split_axis=0, concat_axis=0, tiled=T...  7.3 us
    broadcast_in_dim x5, local copies, waits for them, and re-layouts, body(): jnp.broadcast_to(taps[n][:, :, None], (groups, TAPS * TAPS, TILE, LANES))  3.6 us
    unnamed x16, local copies, waits for them, and re-layouts  3.16 us
  transfers between devices with their start and end apart: 13, of which 6 were waited for; matrix products, arithmetic and copies ran while one was open for 3% of the time, Pallas kernels for 0%

commit v1 on v0

v1 whole, which is shorter than its diff:
```python
import functools

import jax
import jax.numpy as jnp
from jax import lax
from jax.experimental import pallas as pl
from jax.experimental.pallas import tpu as pltpu
from jax.sharding import PartitionSpec as P

LANES = 128
META = 8
TAPS = 7
HALO = 3
SHIFT = 2 * HALO
EDGE = 8
TILE = 16
VMEM_LIMIT = 24 * 1024 * 1024
PACK_LIMIT = 58 * 1024 * 1024
BF16 = jnp.bfloat16
F32 = jnp.float32


def pack_kernel(cap, cols, dest_hbm, foot_hbm, weights_hbm, obs_hbm, send_ref, dest_ref, foot_ref, weights_ref, obs_ref, sems):
    copies = [
        pltpu.make_async_copy(source, target, sems.at[k])
        for k, (source, target) in enumerate(
            (
                (dest_hbm, dest_ref),
                (obs_hbm, obs_ref),
                (foot_hbm, foot_ref),
                (weights_hbm, weights_ref),
            )
        )
    ]
    for copy in copies:
        copy.start()
    devices = send_ref.shape[0]
    obs_rows = obs_ref.shape[0]
    per = LANES // cap
    upper = lax.broadcasted_iota(jnp.int32, (LANES, LANES), 0) <= lax.broadcasted_iota(
        jnp.int32, (LANES, LANES), 1
    )
    upper = jnp.where(upper, 1.0, 0.0).astype(BF16)
    ids = lax.broadcasted_iota(jnp.int32, (devices, obs_rows), 0)
    copies[0].wait()
    member = jnp.where(ids == dest_ref[...], 1.0, 0.0)
    seen = jnp.zeros((devices, 1), F32)
    ranks = []
    for first in range(0, obs_rows, LANES):
        part = member[:, first : first + LANES]
        count = jnp.dot(part.astype(BF16), upper, preferred_element_type=F32) + seen
        ranks.append(jnp.sum((count - 1.0) * part, axis=0, keepdims=True))
        seen = count[:, LANES - 1 :]
    rank = jnp.concatenate(ranks, axis=1).astype(jnp.int32)
    slot = lax.broadcasted_iota(jnp.int32, (cap, obs_rows), 0)
    ranked = jnp.where(slot == rank, 1.0, 0.0).astype(BF16).reshape(cap // TILE, TILE, obs_rows)
    for copy in copies[1:]:
        copy.wait()
    start = foot_ref[0:1, :]
    meta = jnp.concatenate(
        [
            lax.div(start, cols).astype(F32),
            lax.rem(start, cols).astype(F32),
            weights_ref[...].astype(F32),
            jnp.zeros((META - 2 - weights_ref.shape[0], obs_rows), F32),
        ],
        axis=0,
    ).astype(BF16)
    obs = obs_ref[...]
    lane = lax.broadcasted_iota(jnp.int32, (META, LANES), 1)
    count = min(512, devices * cap) // cap
    for first in range(0, devices, count):
        parts = []
        for d in range(first, first + count):
            mine = jnp.broadcast_to(member[d : d + 1], (TILE, obs_rows)).astype(BF16)
            parts.append((ranked * mine[None]).reshape(cap, obs_rows))
        chosen = jnp.concatenate(parts, axis=0)
        feats = jnp.dot(chosen, obs, preferred_element_type=F32).astype(BF16)
        placed = lax.dot_general(
            meta, chosen, (((1,), (1,)), ((), ())), preferred_element_type=F32
        )
        for half in range(feats.shape[1] // LANES):
            piece = feats[:, half * LANES : (half + 1) * LANES].reshape(count, cap, LANES)
            send_ref[first : first + count, half * cap : (half + 1) * cap, :] = piece
        base = send_ref.shape[1] - META
        for chunk in range(count // per):
            values = placed[:, chunk * LANES : (chunk + 1) * LANES]
            turned = [values] + [pltpu.roll(values, k * cap, 1) for k in range(1, per)]
            for own in range(per):
                wide = turned[0]
                for group in range(per):
                    wide = jnp.where(lane // cap == group, turned[(group - own) % per], wide)
                send_ref[first + chunk * per + own, base:, :] = wide.astype(BF16)


def assim_kernel(
    cap, step, got_ref, proj_ref, back_ref, edge_ref, inner_ref, lon_ref, corner_ref
):
    devices, depth, _ = got_ref.shape
    rows, cols, chans = back_ref.shape
    cells = rows * cols
    feats = proj_ref.shape[0]
    per = LANES // cap
    halves = feats // LANES
    lane = lax.broadcasted_iota(jnp.int32, (META, LANES), 1)
    cell = lax.broadcasted_iota(jnp.int32, (cells, LANES), 0)
    total = jnp.zeros((cells, feats), F32)
    for pair in range(0, devices // per, 2):
        maps = []
        blocks = []
        for chunk in (pair, pair + 1):
            meta = got_ref[chunk * per, depth - META :, :].astype(F32)
            for group in range(1, per):
                other = got_ref[chunk * per + group, depth - META :, :].astype(F32)
                meta = jnp.where(lane // cap == group, other, meta)
            start = (meta[0:1] * cols + meta[1:2]).astype(jnp.int32)
            away = cell - start
            away = jnp.where(away < 0, away + cells, away)
            amount = jnp.zeros((cells, LANES), F32)
            for entry in range(4):
                amount = jnp.where(away == entry * step, meta[2 + entry : 3 + entry], amount)
            maps.append(amount.astype(BF16))
            block = got_ref[chunk * per : (chunk + 1) * per]
            blocks.append(
                jnp.concatenate(
                    [
                        block[:, half * cap : (half + 1) * cap, :].reshape(LANES, LANES)
                        for half in range(halves)
                    ],
                    axis=1,
                )
            )
        total = total + jnp.dot(
            jnp.concatenate(maps, axis=1),
            jnp.concatenate(blocks, axis=0),
            preferred_element_type=F32,
        )
    assim = jnp.dot(total.astype(BF16), proj_ref[...], preferred_element_type=F32)
    state = back_ref[...].astype(F32) + assim.reshape(rows, cols, chans)
    state = state.astype(BF16)
    edge_ref[...] = state[rows - SHIFT :]
    inner_ref[...] = state[: rows - SHIFT]
    lon_ref[...] = state[:, cols - EDGE :, :]
    corner_ref[...] = state[rows - SHIFT :, cols - EDGE :, :]


def gelu(x):
    inner = x * (0.7978845608028654 + 0.035677408136300125 * (x * x))
    half = 0.5 * x
    return half + half * jnp.tanh(inner)


def taps_kernel(source_ref, *target_refs):
    @pl.loop(0, source_ref.shape[0])
    def _(k):
        rows = source_ref[k]
        for n, target in enumerate(target_refs):
            for g in range(target.shape[0]):
                row = rows[n : n + 1, g * LANES : (g + 1) * LANES]
                target[g, k] = jnp.broadcast_to(row, (TILE, LANES)).astype(BF16)


def put(wide_ref, row, start, value):
    for g in range(wide_ref.shape[0]):
        wide_ref[g, row, start : start + value.shape[0], :] = value[:, g * LANES : (g + 1) * LANES]


def shifted(wide_ref, taps_in, base, row, target):
    for g in range(wide_ref.shape[0]):
        for r in range(TAPS + 1):
            columns = pl.ds(base + r, TILE, stride=2)
            taps_in[g, r, target] = wide_ref[g, row, columns, :].astype(BF16)


def convolve(taps_in, taps_ref, spread_ref, g, first, count):
    for p in range(2):
        total = None
        for b in range(TAPS):
            seen = taps_in[g, p + b, first : first + count + TAPS - 1]
            part = None
            for a in range(TAPS):
                term = seen[a : a + count] * taps_ref[g, a * TAPS + b]
                part = term if part is None else part + term
            part = part.astype(F32)
            total = part if total is None else total + part
        lanes = pl.ds(pl.multiple_of(g * LANES, LANES), LANES)
        spread_ref[p, first : first + count, :, lanes] = total.astype(BF16)


def finish(taps_in, spread_ref, mix_ref, out_ref, first, count):
    chans = mix_ref.shape[0]
    ones = jnp.ones((chans, LANES), BF16)
    for p in range(2):
        spread = spread_ref[p, first : first + count].reshape(count * TILE, chans)
        power = jnp.dot(spread * spread, ones, preferred_element_type=F32)
        scale = lax.rsqrt(power * (1.0 / chans) + 1e-05)
        mixed = jnp.dot(spread, mix_ref[...], preferred_element_type=F32)
        for g in range(chans // LANES):
            moved = gelu(mixed[:, g * LANES : (g + 1) * LANES] * scale)
            center = taps_in[g, p + HALO, first + HALO : first + HALO + count].astype(F32)
            fresh = center + moved.reshape(count, TILE, LANES)
            for k in range(count):
                out_ref[g, first + k, pl.ds(p, TILE, stride=2), :] = fresh[k]


def row_of(out_ref, y):
    return jnp.concatenate([out_ref[g, y] for g in range(out_ref.shape[0])], axis=1)


def at_last():
    return lax.axis_index("lat") == lax.axis_size("lat") - 1


def inner_kernel(
    shrink,
    edge_in,
    inner_in,
    lon_in,
    taps_ref,
    mix_ref,
    inner_ref,
    lon_ref,
    near_ref,
    wide_ref,
    taps_in,
    spread_ref,
    out_ref,
):
    cols = edge_in.shape[1]
    groups = wide_ref.shape[0]
    own = inner_in.shape[0] - (HALO if shrink else 0)
    rows = own + SHIFT
    count = rows - SHIFT
    side = cols if shrink else 0
    main = 0 if shrink else EDGE
    base = 0 if shrink else EDGE - SHIFT

    def load(ref, place, y):
        put(wide_ref, place, main, ref[y].astype(F32))
        put(wide_ref, place, side, lon_in[place].astype(F32))
        shifted(wide_ref, taps_in, base, place, place)

    @pl.loop(0, SHIFT, unroll=2)
    def _(y):
        load(edge_in, y if shrink else own + y, y)

    @pl.loop(0, own, unroll=2)
    def _(y):
        load(inner_in, y + SHIFT if shrink else y, y)

    near = rows - SHIFT if shrink else 0
    near_ref[...] = taps_in[:, :, near : near + SHIFT]

    @pl.loop(0, groups)
    def _(g):
        convolve(taps_in, taps_ref, spread_ref, g, 0, count)

    finish(taps_in, spread_ref, mix_ref, out_ref, 0, count)
    edge = slice(cols - EDGE, cols) if shrink else slice(0, EDGE)

    @pl.loop(0, count, unroll=2)
    def _(y):
        value = row_of(out_ref, y)
        inner_ref[y] = value.astype(BF16)
        lon_ref[y] = value[edge].astype(BF16)

    if not shrink:

        @pl.when(at_last())
        def _():
            taps_in[:, :, rows:] = jnp.zeros((groups, TAPS + 1, HALO, TILE, LANES), BF16)

            @pl.loop(0, groups)
            def _(g):
                convolve(taps_in, taps_ref, spread_ref, g, count, HALO)

            finish(taps_in, spread_ref, mix_ref, out_ref, count, HALO)

        for k in range(HALO):
            value = row_of(out_ref, count + k)
            inner_ref[count + k] = value.astype(BF16)
            lon_ref[count + k] = value[edge].astype(BF16)


def edge_kernel(
    shrink,
    final,
    inner_in,
    lon_in,
    lat_in,
    corner_in,
    near_ref,
    inner_new,
    lon_new,
    taps_ref,
    mix_ref,
    *refs,
):
    if final:
        state_ref, wide_ref, taps_in, spread_ref, out_ref = refs
    else:
        edge_ref, lon_ref, corner_ref, wide_ref, taps_in, spread_ref, out_ref = refs
    cols = lat_in.shape[1]
    groups = wide_ref.shape[0]
    side = cols if shrink else 0
    main = 0 if shrink else EDGE
    base = 0 if shrink else EDGE - SHIFT
    last = at_last()
    top = lax.axis_index("lat") == 0
    own = SHIFT if not shrink else 0
    for k in range(SHIFT):
        value, beside = lat_in[k].astype(F32), corner_in[k].astype(F32)
        if not shrink:
            value, beside = jnp.where(top, 0.0, value), jnp.where(top, 0.0, beside)
        elif k < HALO:
            rows = lon_in.shape[0] - HALO
            kept = inner_in.shape[0] - HALO
            value = jnp.where(last, inner_in[kept + k].astype(F32), value)
            beside = jnp.where(last, lon_in[rows + k].astype(F32), beside)
        else:
            value, beside = jnp.where(last, 0.0, value), jnp.where(last, 0.0, beside)
        put(wide_ref, k, main, value)
        put(wide_ref, k, side, beside)
        shifted(wide_ref, taps_in, base, k, k if not shrink else k + SHIFT)
    taps_in[:, :, own : own + SHIFT] = near_ref[...]

    @pl.loop(0, groups)
    def _(g):
        convolve(taps_in, taps_ref, spread_ref, g, 0, SHIFT)

    finish(taps_in, spread_ref, mix_ref, out_ref, 0, SHIFT)
    kept = inner_new.shape[0]
    for k in range(SHIFT):
        value = row_of(out_ref, k)
        if final:
            state_ref[kept + k] = value.astype(BF16)
            continue
        if not shrink and k < HALO:
            value = jnp.where(top, 0.0, value)
        value = value.astype(F32)
        edge = value[cols - EDGE :] if shrink else value[:EDGE]
        edge_ref[k] = value.astype(BF16)
        corner_ref[k] = edge.astype(BF16)
        lon_ref[kept + k if shrink else k] = edge.astype(BF16)
    if final:
        state_ref[0:kept] = inner_new[...]
    elif shrink:
        lon_ref[0:kept] = lon_new[...]
    else:
        lon_ref[SHIFT : SHIFT + kept] = lon_new[...]


def call(kernel, out_shape, inputs, scratch=(), limit=VMEM_LIMIT, space=pltpu.VMEM):
    whole = pl.BlockSpec(memory_space=pltpu.VMEM)
    single = isinstance(out_shape, jax.ShapeDtypeStruct)
    return pl.pallas_call(
        kernel,
        out_shape=out_shape,
        in_specs=[pl.BlockSpec(memory_space=space)] * len(inputs),
        out_specs=whole if single else [whole] * len(out_shape),
        scratch_shapes=list(scratch),
        compiler_params=pltpu.CompilerParams(vmem_limit_bytes=limit),
    )(*inputs)


def held(*shape):
    return jax.ShapeDtypeStruct(shape, BF16)


def scratch_of(groups, seen, made, cols, chans):
    return (
        pltpu.VMEM((groups, seen, cols + EDGE, LANES), F32),
        pltpu.VMEM((groups, TAPS + 1, seen, TILE, LANES), BF16),
        pltpu.VMEM((2, made, TILE, chans), BF16),
        pltpu.VMEM((groups, made, cols, LANES), F32),
    )


def layer(state, lon_out, corner_out, taps, mix, shrink, final):
    edge, inner = state
    lat_in, lon_in, corner_in = exchange((edge, lon_out, corner_out), not shrink)
    cols, chans = edge.shape[1:]
    groups = chans // LANES
    rows = inner.shape[0] + SHIFT - (HALO if shrink else 0)
    spare = 0 if shrink else HALO
    made = rows - SHIFT + spare
    inner_new, lon_new, near = call(
        functools.partial(inner_kernel, shrink),
        (
            held(made, cols, chans),
            held(made, EDGE, chans),
            held(groups, TAPS + 1, SHIFT, TILE, LANES),
        ),
        (edge, inner, lon_in, taps, mix),
        scratch_of(groups, rows + spare, made, cols, chans),
    )
    if final:
        outs = held(made + SHIFT, cols, chans)
    else:
        outs = (
            held(SHIFT, cols, chans),
            held(made + SHIFT, EDGE, chans),
            held(SHIFT, EDGE, chans),
        )
    outs = call(
        functools.partial(edge_kernel, shrink, final),
        outs,
        (inner, lon_in, lat_in, corner_in, near, inner_new, lon_new, taps, mix),
        scratch_of(groups, 2 * SHIFT, SHIFT, cols, chans),
    )
    if final:
        return outs
    edge, lon_out, corner_out = outs
    return (edge, inner_new), lon_out, corner_out


def exchange(pieces, forward):
    lat, lon, corner = pieces
    count_lat = lax.axis_size("lat")
    count_lon = lax.axis_size("lon")
    along = [(i, (i + 1) % count_lat) for i in range(count_lat)]
    around = [(j, (j + 1) % count_lon) for j in range(count_lon)]
    across = [
        (i * count_lon + j, ni * count_lon + nj) for i, ni in along for j, nj in around
    ]
    if not forward:
        along, around, across = ([(t, s) for s, t in p] for p in (along, around, across))
    return (
        lax.ppermute(lat, "lat", along),
        lax.ppermute(lon, "lon", around),
        lax.ppermute(corner, ("lat", "lon"), across),
    )


def body(
    background, observations, destination, footprint, weights, obs_proj, depth_w, point_w, gains
):
    rows, cols, chans = background.shape
    devices = lax.axis_size("lat") * lax.axis_size("lon")
    obs_rows, feats = observations.shape
    cap = 2 * obs_rows // devices
    depth = cap * (feats // LANES) + META
    foot_count = footprint.shape[1]
    send = call(
        functools.partial(pack_kernel, cap, cols),
        jax.ShapeDtypeStruct((devices, depth, LANES), BF16),
        (destination.T, footprint.T, weights.T, observations),
        (
            pltpu.VMEM((1, obs_rows), jnp.int32),
            pltpu.VMEM((foot_count, obs_rows), jnp.int32),
            pltpu.VMEM((foot_count, obs_rows), BF16),
            pltpu.VMEM((obs_rows, feats), BF16),
            pltpu.SemaphoreType.DMA((4,)),
        ),
        PACK_LIMIT,
        pltpu.HBM,
    )
    got = lax.all_to_all(send, ("lat", "lon"), split_axis=0, concat_axis=0, tiled=True)
    layers = depth_w.shape[0]
    groups = chans // LANES
    taps = call(
        taps_kernel,
        [held(groups, TAPS * TAPS, TILE, LANES)] * layers,
        (depth_w.transpose(1, 2, 0, 3).reshape(TAPS * TAPS, layers, chans),),
    )
    mix = [(gains[n][:, None] * point_w[n].astype(F32)).astype(BF16) for n in range(layers)]
    got, taps, mix = lax.optimization_barrier((got, taps, mix))
    edge, inner, lon_out, corner_out = call(
        functools.partial(assim_kernel, cap, cols + 1),
        (
            held(SHIFT, cols, chans),
            held(rows - SHIFT, cols, chans),
            held(rows, EDGE, chans),
            held(SHIFT, EDGE, chans),
        ),
        (got, obs_proj, background),
    )
    state = (edge, inner)
    for n in range(layers - 1):
        state, lon_out, corner_out = layer(
            state, lon_out, corner_out, taps[n], mix[n], n % 2 == 1, False
        )
    n = layers - 1
    return layer(state, lon_out, corner_out, taps[n], mix[n], n % 2 == 1, True)


def solution(mesh):
    placed = (
        P("lat", "lon", None),
        P(("lat", "lon"), None),
        P(("lat", "lon"), None),
        P(("lat", "lon"), None),
        P(("lat", "lon"), None),
        P(),
        P(),
        P(),
        P(),
    )
    return jax.shard_map(
        body, mesh=mesh, in_specs=placed, out_specs=P("lat", "lon", None), check_vma=False
    )
```

time: 112 us -> 98.2 us (0.88)
  waiting for transfers between devices: 48.2 us -> 38.8 us
  local copies, waits for them, and re-layouts: 6.91 us -> 4.7 us
  starting transfers between devices: 19.4 us -> 18.1 us
    ppermute x4, waiting for transfers between devices: 21.7 us -> 0.01 us  [exchange(): lax.ppermute(corner, ('lat', 'lon'), across)]
    ppermute x4, waiting for transfers between devices: 0.01 us -> 15.9 us  [exchange(): lax.ppermute(lon, 'lon', around)]
    broadcast_in_dim x5 -> x0, local copies, waits for them, and re-layouts: 3.6 us -> none  [body(): jnp.broadcast_to(taps[n][:, :, None], (groups, TAPS * TAPS, TILE, LANES))]
    all_to_all x1, waiting for transfers between devices: 26.1 us -> 22.9 us  [body(): lax.all_to_all(send, ('lat', 'lon'), split_axis=0, concat_axis=0, tiled=T...]
    unnamed x16 -> x24, local copies, waits for them, and re-layouts: 3.16 us -> 4.7 us
    ppermute x4, starting transfers between devices: 2.02 us -> 0.63 us  [exchange(): lax.ppermute(lon, 'lon', around)]
    pallas_call x6 -> x11, Pallas kernels: 34.4 us -> 34 us  [call(): pl.pallas_call(kernel, out_shape=out_shape, in_specs=[pl.BlockSpec(memory...]
  transfers between devices with their start and end apart: 13 -> 13, of which waited for: 6 -> 5; matrix products, arithmetic and copies ran while one was open for 3% -> 2% of each run, Pallas kernels for 0% -> 17%
where the time goes in v1:
time: 98.2 us; the launch traced here: 97.9 us
  waiting for transfers between devices  38.8 us (40%)
  Pallas kernels  34 us (35%)
  starting transfers between devices  18.1 us (18%)
  local copies, waits for them, and re-layouts  4.7 us (5%)
  other arithmetic  2.03 us (2%)
    pallas_call x11, Pallas kernels, call(): pl.pallas_call(kernel, out_shape=out_shape, in_specs=[pl.BlockSpec(memory...  34 us
    all_to_all x1, waiting for transfers between devices, body(): lax.all_to_all(send, ('lat', 'lon'), split_axis=0, concat_axis=0, tiled=T...  22.9 us
    ppermute x4, waiting for transfers between devices, exchange(): lax.ppermute(lon, 'lon', around)  15.9 us
    ppermute x4, starting transfers between devices, exchange(): lax.ppermute(lat, 'lat', along)  8.54 us
    all_to_all x1, starting transfers between devices, body(): lax.all_to_all(send, ('lat', 'lon'), split_axis=0, concat_axis=0, tiled=T...  7.3 us
    unnamed x24, local copies, waits for them, and re-layouts  4.7 us
    convert_element_type x1, other arithmetic, body(): (gains[n][:, None] * point_w[n].astype(F32)).astype(BF16)  2.03 us
  transfers between devices with their start and end apart: 13, of which 5 were waited for; matrix products, arithmetic and copies ran while one was open for 2% of the time, Pallas kernels for 17%

profile of v1, /device:TPU:0, one launch (start us, length us, event | category | flops | bytes accessed | tf_op | source)
XLA Modules:
  0.0 97.9 jit_solution(12545207005778498910)
XLA Ops:
  0.0 4.8 %shard_map.91 = bf16[32,136,128]{2,1,0:T(8,128)(2,1)} custom-call(s32[1,1024]{1,0:T(1,128)} %bitcast.29, s32[4,1024]{1,0:T(4,128)} %bitcast.23, bf16[4,1024]{1,0:T(4,128)(2,1)} %bitcast.24, bf16[1024,256]{1,0:T(8,128)(2,1)} %obs_hbm.1), custom_call_target="tpu_custom_call" | custom-call | tf_op jit(solution)/shard_map/pallas_call | solution.py:356
  4.8 7.3 %all-to-all-start = ((bf16[32,136,128]{2,1,0:T(8,128)(2,1)}), bf16[32,136,128]{2,1,0:T(8,128)(2,1)S(1)}, u32[]{:S(2)}, u32[]{:S(2)}) async-start(bf16[32,136,128]{2,1,0:T(8,128)(2,1)} %shard_map.91), calls=%async_computation | async-start | bytes 2228224 | tf_op jit(solution)/shard_map/all_to_all | solution.py:458
  13.4 0.9 copy-done.2
  14.3 0.9 copy-done.4
  15.2 0.9 copy-done.6
  16.1 2.0 %fusion = (bf16[512,512]{1,0:T(8,128)(2,1)S(1)}, bf16[512,512]{1,0:T(8,128)(2,1)S(1)}, bf16[512,512]{1,0:T(8,128)(2,1)S(1)}, bf16[512,512]{1,0:T(8,128)(2,1)S(1)}) fusion(bf16[4,512,512]{2,1,0:T(8,128)(2,1)} %param.16, f32[512]{0:T(512)S(1)} %bitcast.25, f32[512]{0:T(512)S(1)} %bitcast.26, f32[512]{0:T(512)S(1)} %bitcast.27, f32[512]{0:T(512)S(1)} %bitcast.28), kind=kLoop, calls=%fused_computation.1 | loop fusion | flops 3145728 | bytes 4202496 | tf_op jit(solution)/shard_map/convert_element_type | solution.py:466
  18.1 22.9 %all-to-all-done.got_ref = bf16[32,136,128]{2,1,0:T(8,128)(2,1)S(1)} async-done(((bf16[32,136,128]{2,1,0:T(8,128)(2,1)}), bf16[32,136,128]{2,1,0:T(8,128)(2,1)S(1)}, u32[]{:S(2)}, u32[]{:S(2)}) %all-to-all-start) | async-done | bytes 1114144 | tf_op jit(solution)/shard_map/all_to_all | solution.py:458
  41.1 1.1 %copy-done.8 = bf16[16,32,512]{2,1,0:T(8,128)(2,1)S(1)} copy-done((bf16[16,32,512]{2,1,0:T(8,128)(2,1)S(1)}, bf16[16,32,512]{2,1,0:T(8,128)(2,1)}, u32[]{:S(2)}) %copy-start.8) | copy-done | bytes 524312
  42.2 2.2 %shard_map.93 = (bf16[6,32,512]{2,1,0:T(8,128)(2,1)S(1)}, bf16[10,32,512]{2,1,0:T(8,128)(2,1)S(1)}, bf16[16,8,512]{2,1,0:T(8,128)(2,1)S(1)}, bf16[6,8,512]{2,1,0:T(8,128)(2,1)S(1)}) custom-call(bf16[32,136,128]{2,1,0:T(8,128)(2,1)S(1)} %all-to-all-done.got_ref, bf16[256,512]{1,0:T(8,128)(2,1)S(1)} %copy-done.10, bf16[16,32,512]{2,1,0:T(8,128)(2,1)S(1)} %copy-done.8), custom_call_target="tpu_custom_call" | custom-call | tf_op jit(solution)/shard_map/pallas_call | solution.py:356
  45.1 1.1 %collective-permute-start.2 = (bf16[6,8,512]{2,1,0:T(8,128)(2,1)S(1)}, bf16[6,8,512]{2,1,0:T(8,128)(2,1)S(1)}, u32[]{:S(2)}, u32[]{:S(2)}) collective-permute-start(bf16[6,8,512]{2,1,0:T(8,128)(2,1)S(1)} %get-tuple-element.54), channel_id=1, source_target_pairs={{0,9},{1,10},{2,11},{3,12},{4,13},{5,14},{6,15},{7,8},{8,17},{9,18... | collective-permute-start | bytes 147464 | tf_op jit(solution)/shard_map/ppermute | solution.py:431
  46.1 4.6 %collective-permute-done.lon_in = bf16[16,8,512]{2,1,0:T(8,128)(2,1)S(1)} collective-permute-done((bf16[16,8,512]{2,1,0:T(8,128)(2,1)S(1)}, bf16[16,8,512]{2,1,0:T(8,128)(2,1)S(1)}, u32[]{:S(2)}, u32[]{:S(2)}) %collective-permute-start) | collective-permute-done | bytes 131104 | tf_op jit(solution)/shard_map/ppermute | solution.py:430
  50.7 3.9 %shard_map.94 = (bf16[13,32,512]{2,1,0:T(8,128)(2,1)S(1)}, bf16[13,8,512]{2,1,0:T(8,128)(2,1)S(1)}, bf16[4,8,6,16,128]{4,3,2,1,0:T(8,128)(2,1)S(1)}) custom-call(bf16[6,32,512]{2,1,0:T(8,128)(2,1)S(1)} %get-tuple-element.48.edge_in, bf16[10,32,512]{2,1,0:T(8,128)(2,1)S(1)} %get-tuple-element.49.inner_in, ...), custom_call_target="tpu_custom_call" | custom-call | tf_op jit(solution)/shard_map/pallas_call | solution.py:356
  54.7 2.5 %shard_map.95 = (bf16[6,32,512]{2,1,0:T(8,128)(2,1)S(1)}, bf16[19,8,512]{2,1,0:T(8,128)(2,1)S(1)}, bf16[6,8,512]{2,1,0:T(8,128)(2,1)S(1)}) custom-call(bf16[10,32,512]{2,1,0:T(8,128)(2,1)S(1)} %get-tuple-element.49.inner_in, bf16[16,8,512]{2,1,0:T(8,128)(2,1)S(1)} %collective-permute-done.lon_in, bf16[6,32,512]{2,1,0:T(8,128)(2,1)S(1)} %collective-permute-done.1.lat_in, ...), custom_call_target="tpu_custom_call" | custom-call | tf_op jit(solution)/shard_map/pallas_call | solution.py:356
  57.2 4.3 %collective-permute-start.4 = (bf16[6,32,512]{2,1,0:T(8,128)(2,1)S(1)}, bf16[6,32,512]{2,1,0:T(8,128)(2,1)S(1)}, u32[]{:S(2)}, u32[]{:S(2)}) collective-permute-start(bf16[6,32,512]{2,1,0:T(8,128)(2,1)S(1)} %get-tuple-element.58.edge_in), channel_id=1, source_target_pairs={{8,0},{16,8},{24,16},{0,24},{9,1},{17,9},{25,17},{1,25},{10,2},{18... | collective-permute-start | bytes 589832 | tf_op jit(solution)/shard_map/ppermute | solution.py:429
  61.5 2.7 %collective-permute-done.3.lon_in = bf16[19,8,512]{2,1,0:T(8,128)(2,1)S(1)} collective-permute-done((bf16[19,8,512]{2,1,0:T(8,128)(2,1)S(1)}, bf16[19,8,512]{2,1,0:T(8,128)(2,1)S(1)}, u32[]{:S(2)}, u32[]{:S(2)}) %collective-permute-start.3) | collective-permute-done | bytes 155680 | tf_op jit(solution)/shard_map/ppermute | solution.py:430
  64.2 4.0 %shard_map.96 = (bf16[10,32,512]{2,1,0:T(8,128)(2,1)S(1)}, bf16[10,8,512]{2,1,0:T(8,128)(2,1)S(1)}, bf16[4,8,6,16,128]{4,3,2,1,0:T(8,128)(2,1)S(1)}) custom-call(bf16[6,32,512]{2,1,0:T(8,128)(2,1)S(1)} %get-tuple-element.58.edge_in, bf16[13,32,512]{2,1,0:T(8,128)(2,1)S(1)} %get-tuple-element.53.inner_new.inner_in, ...), custom_call_target="tpu_custom_call" | custom-call | tf_op jit(solution)/shard_map/pallas_call | solution.py:356
  68.3 2.5 %shard_map.97 = (bf16[6,32,512]{2,1,0:T(8,128)(2,1)S(1)}, bf16[16,8,512]{2,1,0:T(8,128)(2,1)S(1)}, bf16[6,8,512]{2,1,0:T(8,128)(2,1)S(1)}) custom-call(bf16[13,32,512]{2,1,0:T(8,128)(2,1)S(1)} %get-tuple-element.53.inner_new.inner_in, bf16[19,8,512]{2,1,0:T(8,128)(2,1)S(1)} %collective-permute-done.3.lon_in, ...), custom_call_target="tpu_custom_call" | custom-call | tf_op jit(solution)/shard_map/pallas_call | solution.py:356
  71.5 5.8 %collective-permute-done.6.lon_in = bf16[16,8,512]{2,1,0:T(8,128)(2,1)S(1)} collective-permute-done((bf16[16,8,512]{2,1,0:T(8,128)(2,1)S(1)}, bf16[16,8,512]{2,1,0:T(8,128)(2,1)S(1)}, u32[]{:S(2)}, u32[]{:S(2)}) %collective-permute-start.6) | collective-permute-done | bytes 131104 | tf_op jit(solution)/shard_map/ppermute | solution.py:430
  77.3 3.9 %shard_map.98 = (bf16[13,32,512]{2,1,0:T(8,128)(2,1)S(1)}, bf16[13,8,512]{2,1,0:T(8,128)(2,1)S(1)}, bf16[4,8,6,16,128]{4,3,2,1,0:T(8,128)(2,1)S(1)}) custom-call(bf16[6,32,512]{2,1,0:T(8,128)(2,1)S(1)} %get-tuple-element.65.edge_in, bf16[10,32,512]{2,1,0:T(8,128)(2,1)S(1)} %get-tuple-element.63.inner_new.inner_in, ...), custom_call_target="tpu_custom_call" | custom-call | tf_op jit(solution)/shard_map/pallas_call | solution.py:356
  81.2 2.5 %shard_map.99 = (bf16[6,32,512]{2,1,0:T(8,128)(2,1)S(1)}, bf16[19,8,512]{2,1,0:T(8,128)(2,1)S(1)}, bf16[6,8,512]{2,1,0:T(8,128)(2,1)S(1)}) custom-call(bf16[10,32,512]{2,1,0:T(8,128)(2,1)S(1)} %get-tuple-element.63.inner_new.inner_in, bf16[16,8,512]{2,1,0:T(8,128)(2,1)S(1)} %collective-permute-done.6.lon_in, ...), custom_call_target="tpu_custom_call" | custom-call | tf_op jit(solution)/shard_map/pallas_call | solution.py:356
  83.7 4.1 %collective-permute-start.10 = (bf16[6,32,512]{2,1,0:T(8,128)(2,1)S(1)}, bf16[6,32,512]{2,1,0:T(8,128)(2,1)S(1)}, u32[]{:S(2)}, u32[]{:S(2)}) collective-permute-start(bf16[6,32,512]{2,1,0:T(8,128)(2,1)S(1)} %get-tuple-element.74.edge_in), channel_id=1, source_target_pairs={{8,0},{16,8},{24,16},{0,24},{9,1},{17,9},{25,17},{1,25},{10,2},{18... | collective-permute-start | bytes 589832 | tf_op jit(solution)/shard_map/ppermute | solution.py:429
  87.9 2.7 %collective-permute-done.9.lon_in = bf16[19,8,512]{2,1,0:T(8,128)(2,1)S(1)} collective-permute-done((bf16[19,8,512]{2,1,0:T(8,128)(2,1)S(1)}, bf16[19,8,512]{2,1,0:T(8,128)(2,1)S(1)}, u32[]{:S(2)}, u32[]{:S(2)}) %collective-permute-start.9) | collective-permute-done | bytes 155680 | tf_op jit(solution)/shard_map/ppermute | solution.py:430
  90.6 4.0 %shard_map.100 = (bf16[10,32,512]{2,1,0:T(8,128)(2,1)S(1)}, bf16[10,8,512]{2,1,0:T(8,128)(2,1)S(1)}, bf16[4,8,6,16,128]{4,3,2,1,0:T(8,128)(2,1)S(1)}) custom-call(bf16[6,32,512]{2,1,0:T(8,128)(2,1)S(1)} %get-tuple-element.74.edge_in, bf16[13,32,512]{2,1,0:T(8,128)(2,1)S(1)} %get-tuple-element.69.inner_new.inner_in, ...), custom_call_target="tpu_custom_call" | custom-call | tf_op jit(solution)/shard_map/pallas_call | solution.py:356
  94.7 3.3 %shard_map.101 = bf16[16,32,512]{2,1,0:T(8,128)(2,1)} custom-call(bf16[13,32,512]{2,1,0:T(8,128)(2,1)S(1)} %get-tuple-element.69.inner_new.inner_in, bf16[19,8,512]{2,1,0:T(8,128)(2,1)S(1)} %collective-permute-done.9.lon_in, bf16[6,32,512]{2,1,0:T(8,128)(2,1)S(1)} %collective-permute-done.10.lat_in, ...), custom_call_target="tpu_custom_call" | custom-call | tf_op jit(solution)/shard_map/pallas_call | solution.py:356
  (39 shorter events, 2.7 us)
Async XLA Ops:
  0.0 12.1 %copy-start.9 = (f32[4,7,7,512]{3,0,2,1:T(4,128)S(1)}, f32[4,7,7,512]{3,0,2,1:T(4,128)}, u32[]{:S(2)}) copy-start(f32[4,7,7,512]{3,0,2,1:T(4,128)} %param.15) | copy-start | bytes 1204228
  0.0 16.1 %copy-start.11 = (f32[4,512]{1,0:T(4,128)S(1)}, f32[4,512]{1,0:T(4,128)}, u32[]{:S(2)}) copy-start(f32[4,512]{1,0:T(4,128)} %param.17) | copy-start | bytes 24580
  4.8 36.3 %all-to-all-start = ((bf16[32,136,128]{2,1,0:T(8,128)(2,1)}), bf16[32,136,128]{2,1,0:T(8,128)(2,1)S(1)}, u32[]{:S(2)}, u32[]{:S(2)}) async-start(bf16[32,136,128]{2,1,0:T(8,128)(2,1)} %shard_map.91), calls=%async_computation | async-start | bytes 2228224 | tf_op jit(solution)/shard_map/all_to_all | solution.py:458
  12.5 0.9 copy-start
  13.4 0.9 copy-start.2
  15.2 0.9 copy-start.6
  16.1 25.0 %copy-start.10 = (bf16[256,512]{1,0:T(8,128)(2,1)S(1)}, bf16[256,512]{1,0:T(8,128)(2,1)}, u32[]{:S(2)}) copy-start(bf16[256,512]{1,0:T(8,128)(2,1)} %proj_ref.1) | copy-start | bytes 786436
  41.1 9.7 %copy-start.5 = (bf16[4,49,16,128]{3,2,1,0:T(8,128)(2,1)S(1)}, bf16[4,49,16,128]{3,2,1,0:T(8,128)(2,1)}, u32[]{:S(2)}) copy-start(bf16[4,49,16,128]{3,2,1,0:T(8,128)(2,1)} %copy-done.4) | copy-start | bytes 2408452
  41.1 1.1 %copy-start.8 = (bf16[16,32,512]{2,1,0:T(8,128)(2,1)S(1)}, bf16[16,32,512]{2,1,0:T(8,128)(2,1)}, u32[]{:S(2)}) copy-start(bf16[16,32,512]{2,1,0:T(8,128)(2,1)} %back_ref.1) | copy-start | bytes 1572868
  44.4 10.3 %collective-permute-start.1 = (bf16[6,32,512]{2,1,0:T(8,128)(2,1)S(1)}, bf16[6,32,512]{2,1,0:T(8,128)(2,1)S(1)}, u32[]{:S(2)}, u32[]{:S(2)}) collective-permute-start(bf16[6,32,512]{2,1,0:T(8,128)(2,1)S(1)} %get-tuple-element.48.edge_in), channel_id=1, source_target_pairs={{0,8},{8,16},{16,24},{24,0},{1,9},{9,17},{17,25},{25,1},{2,10},{10... | collective-permute-start | bytes 589832 | tf_op jit(solution)/shard_map/ppermute | solution.py:429
  44.5 6.2 %collective-permute-start = (bf16[16,8,512]{2,1,0:T(8,128)(2,1)S(1)}, bf16[16,8,512]{2,1,0:T(8,128)(2,1)S(1)}, u32[]{:S(2)}, u32[]{:S(2)}) collective-permute-start(bf16[16,8,512]{2,1,0:T(8,128)(2,1)S(1)} %get-tuple-element.50), channel_id=1, source_target_pairs={{0,1},{1,2},{2,3},{3,4},{4,5},{5,6},{6,7},{7,0},{8,9},{9,10},{10,1... | collective-permute-start | bytes 393224 | tf_op jit(solution)/shard_map/ppermute | solution.py:430
  45.1 9.6 %collective-permute-start.2 = (bf16[6,8,512]{2,1,0:T(8,128)(2,1)S(1)}, bf16[6,8,512]{2,1,0:T(8,128)(2,1)S(1)}, u32[]{:S(2)}, u32[]{:S(2)}) collective-permute-start(bf16[6,8,512]{2,1,0:T(8,128)(2,1)S(1)} %get-tuple-element.54), channel_id=1, source_target_pairs={{0,9},{1,10},{2,11},{3,12},{4,13},{5,14},{6,15},{7,8},{8,17},{9,18... | collective-permute-start | bytes 147464 | tf_op jit(solution)/shard_map/ppermute | solution.py:431
  54.7 9.6 %copy-start.3 = (bf16[4,49,16,128]{3,2,1,0:T(8,128)(2,1)S(1)}, bf16[4,49,16,128]{3,2,1,0:T(8,128)(2,1)}, u32[]{:S(2)}) copy-start(bf16[4,49,16,128]{3,2,1,0:T(8,128)(2,1)} %copy-done.2) | copy-start | bytes 2408452
  57.2 11.1 %collective-permute-start.4 = (bf16[6,32,512]{2,1,0:T(8,128)(2,1)S(1)}, bf16[6,32,512]{2,1,0:T(8,128)(2,1)S(1)}, u32[]{:S(2)}, u32[]{:S(2)}) collective-permute-start(bf16[6,32,512]{2,1,0:T(8,128)(2,1)S(1)} %get-tuple-element.58.edge_in), channel_id=1, source_target_pairs={{8,0},{16,8},{24,16},{0,24},{9,1},{17,9},{25,17},{1,25},{10,2},{18... | collective-permute-start | bytes 589832 | tf_op jit(solution)/shard_map/ppermute | solution.py:429
  61.5 2.8 %collective-permute-start.3 = (bf16[19,8,512]{2,1,0:T(8,128)(2,1)S(1)}, bf16[19,8,512]{2,1,0:T(8,128)(2,1)S(1)}, u32[]{:S(2)}, u32[]{:S(2)}) collective-permute-start(bf16[19,8,512]{2,1,0:T(8,128)(2,1)S(1)} %get-tuple-element.57), channel_id=1, source_target_pairs={{1,0},{2,1},{3,2},{4,3},{5,4},{6,5},{7,6},{0,7},{9,8},{10,9},{11,1... | collective-permute-start | bytes 466952 | tf_op jit(solution)/shard_map/ppermute | solution.py:430
  61.5 6.8 %collective-permute-start.5 = (bf16[6,8,512]{2,1,0:T(8,128)(2,1)S(1)}, bf16[6,8,512]{2,1,0:T(8,128)(2,1)S(1)}, u32[]{:S(2)}, u32[]{:S(2)}) collective-permute-start(bf16[6,8,512]{2,1,0:T(8,128)(2,1)S(1)} %get-tuple-element.59), channel_id=1, source_target_pairs={{9,0},{10,1},{11,2},{12,3},{13,4},{14,5},{15,6},{8,7},{17,8},{18,9... | collective-permute-start | bytes 147464 | tf_op jit(solution)/shard_map/ppermute | solution.py:431
  68.3 9.0 %copy-start.1 = (bf16[4,49,16,128]{3,2,1,0:T(8,128)(2,1)S(1)}, bf16[4,49,16,128]{3,2,1,0:T(8,128)(2,1)}, u32[]{:S(2)}) copy-start(bf16[4,49,16,128]{3,2,1,0:T(8,128)(2,1)} %copy-done) | copy-start | bytes 2408452
  70.8 10.4 %collective-permute-start.7 = (bf16[6,32,512]{2,1,0:T(8,128)(2,1)S(1)}, bf16[6,32,512]{2,1,0:T(8,128)(2,1)S(1)}, u32[]{:S(2)}, u32[]{:S(2)}) collective-permute-start(bf16[6,32,512]{2,1,0:T(8,128)(2,1)S(1)} %get-tuple-element.65.edge_in), channel_id=1, source_target_pairs={{0,8},{8,16},{16,24},{24,0},{1,9},{9,17},{17,25},{25,1},{2,10},{10... | collective-permute-start | bytes 589832 | tf_op jit(solution)/shard_map/ppermute | solution.py:429
  70.9 6.4 %collective-permute-start.6 = (bf16[16,8,512]{2,1,0:T(8,128)(2,1)S(1)}, bf16[16,8,512]{2,1,0:T(8,128)(2,1)S(1)}, u32[]{:S(2)}, u32[]{:S(2)}) collective-permute-start(bf16[16,8,512]{2,1,0:T(8,128)(2,1)S(1)} %get-tuple-element.66), channel_id=1, source_target_pairs={{0,1},{1,2},{2,3},{3,4},{4,5},{5,6},{6,7},{7,0},{8,9},{9,10},{10,1... | collective-permute-start | bytes 393224 | tf_op jit(solution)/shard_map/ppermute | solution.py:430
  70.9 10.3 %collective-permute-start.8 = (bf16[6,8,512]{2,1,0:T(8,128)(2,1)S(1)}, bf16[6,8,512]{2,1,0:T(8,128)(2,1)S(1)}, u32[]{:S(2)}, u32[]{:S(2)}) collective-permute-start(bf16[6,8,512]{2,1,0:T(8,128)(2,1)S(1)} %get-tuple-element.70), channel_id=1, source_target_pairs={{0,9},{1,10},{2,11},{3,12},{4,13},{5,14},{6,15},{7,8},{8,17},{9,18... | collective-permute-start | bytes 147464 | tf_op jit(solution)/shard_map/ppermute | solution.py:431
  81.2 9.4 %copy-start.7 = (bf16[4,49,16,128]{3,2,1,0:T(8,128)(2,1)S(1)}, bf16[4,49,16,128]{3,2,1,0:T(8,128)(2,1)}, u32[]{:S(2)}) copy-start(bf16[4,49,16,128]{3,2,1,0:T(8,128)(2,1)} %copy-done.6) | copy-start | bytes 2408452
  83.7 10.9 %collective-permute-start.10 = (bf16[6,32,512]{2,1,0:T(8,128)(2,1)S(1)}, bf16[6,32,512]{2,1,0:T(8,128)(2,1)S(1)}, u32[]{:S(2)}, u32[]{:S(2)}) collective-permute-start(bf16[6,32,512]{2,1,0:T(8,128)(2,1)S(1)} %get-tuple-element.74.edge_in), channel_id=1, source_target_pairs={{8,0},{16,8},{24,16},{0,24},{9,1},{17,9},{25,17},{1,25},{10,2},{18... | collective-permute-start | bytes 589832 | tf_op jit(solution)/shard_map/ppermute | solution.py:429
  87.9 2.8 %collective-permute-start.9 = (bf16[19,8,512]{2,1,0:T(8,128)(2,1)S(1)}, bf16[19,8,512]{2,1,0:T(8,128)(2,1)S(1)}, u32[]{:S(2)}, u32[]{:S(2)}) collective-permute-start(bf16[19,8,512]{2,1,0:T(8,128)(2,1)S(1)} %get-tuple-element.73), channel_id=1, source_target_pairs={{1,0},{2,1},{3,2},{4,3},{5,4},{6,5},{7,6},{0,7},{9,8},{10,9},{11,1... | collective-permute-start | bytes 466952 | tf_op jit(solution)/shard_map/ppermute | solution.py:430
  87.9 6.8 %collective-permute-start.11 = (bf16[6,8,512]{2,1,0:T(8,128)(2,1)S(1)}, bf16[6,8,512]{2,1,0:T(8,128)(2,1)S(1)}, u32[]{:S(2)}, u32[]{:S(2)}) collective-permute-start(bf16[6,8,512]{2,1,0:T(8,128)(2,1)S(1)} %get-tuple-element.75), channel_id=1, source_target_pairs={{9,0},{10,1},{11,2},{12,3},{13,4},{14,5},{15,6},{8,7},{17,8},{18,9... | collective-permute-start | bytes 147464 | tf_op jit(solution)/shard_map/ppermute | solution.py:431
  (1 other events, 0.9 us)
